TPU v7x, 256 devices: a whole 4x4x8 slice. The times are simulated.
256 devices in a mesh: tm: 64 (over x, z, y_hi), rec: 4 (over y_lo, core).
Axes of the slice: x: 4, y: 4 (y_hi: 2, y_lo: 2; y = y_hi * 2 + y_lo), z: 8, core: 2. Of those that a mesh axis runs over, the one named last changes fastest.
Arguments:
- frames: bfloat16 [12, 8192, 1536], P('rec', 'tm'), parts along dimension 0, may hold values from -6 to 6
- time_starts: int32 [12, 2], P('rec'), parts along dimension 0, may hold values from 0 to 8191
- time_widths: int32 [12, 2], P('rec'), parts along dimension 0, may hold values from 0 to 40
- freq_starts: int32 [12, 2], P('rec'), parts along dimension 0, may hold values from 0 to 1535
- freq_widths: int32 [12, 2], P('rec'), parts along dimension 0, may hold values from 0 to 192
- lengths: int32 [12], P('rec'), parts along dimension 0, may hold values from 4096 to 8192, as said below
- w_query: bfloat16 [1536, 768], replicated, may hold values from -4 to 4
- w_key: bfloat16 [1536, 768], replicated, may hold values from -4 to 4
- w_value: bfloat16 [1536, 768], replicated, may hold values from -0.15625 to 0.15625
- w_out: bfloat16 [768, 1536], replicated, may hold values from -0.21875 to 0.21875
- attn_gain: float32 [1536], replicated, may hold values from 0.1 to 1.9
- conv_gain: float32 [1536], replicated, may hold values from 0.1 to 1.9
- conv_kernel: float32 [31, 1536], replicated, may hold values from -2 to 2
- conv_scale: float32 [1536], replicated, may hold values from 0.3 to 3
Outputs:
- layer_out: bfloat16 [12, 8192, 1536], P('rec', 'tm'), parts along dimension 0
There are 4 independent parts, one for each index of `rec`. A program takes and returns all parts, laid end to end along the dimension named above; an argument that names none is the same for every part. Nothing has to cross between parts.
Inputs may be any that keep to these rules, and one draw needn't show every extreme that they name: `lengths`: at least half of each recording is valid; in every part one recording is valid to its end and one has exactly 4096 valid frames.
All inputs are finite; a program needn't handle non-finite values.
Results may differ from a plain program's by a relative error of at most 0.0065.
Values may be sent and summed in bfloat16 or wider, within the bound.
A program may use at most 64 MiB of HBM per device.

v0:
```python
import jax
import jax.numpy as jnp
from jax import lax
from jax.sharding import PartitionSpec as P

HSIZE = 64


def shifted(block, axis, distance):
    devices = range(lax.axis_size(axis))
    route = [(i - distance, i) for i in devices if i - distance in devices]
    return lax.ppermute(block, axis, route)


def padded_2(cells, sides, width):
    for axis, dim in sides:
        count = lax.axis_size(axis)
        ends = count - 1
        head = lax.slice_in_dim(cells, 0, width, axis=dim)
        tail = lax.slice_in_dim(cells, cells.shape[dim] - width, cells.shape[dim], axis=dim)
        cells = jnp.concatenate(
            [
                lax.ppermute(tail, axis, [(i, (i + 1) % count) for i in range(ends)]),
                cells,
                lax.ppermute(head, axis, [((i + 1) % count, i) for i in range(ends)]),
            ],
            axis=dim,
        )
    return cells


def keep_mask(starts, widths, places):
    inside = (places[None, None, :] >= starts[:, :, None]) & (
        places[None, None, :] < starts[:, :, None] + widths[:, :, None]
    )
    return 1.0 - jnp.any(inside, axis=1).astype(jnp.float32)


def layer_norm(values, gain):
    values = values.astype(jnp.float32)
    center = jnp.mean(values, axis=-1, keepdims=True)
    spread = jnp.mean((values - center) ** 2, axis=-1, keepdims=True)
    return (values - center) * lax.rsqrt(spread + 1e-05) * gain


def body(
    frames,
    time_starts,
    time_widths,
    freq_starts,
    freq_widths,
    lengths,
    w_query,
    w_key,
    w_value,
    w_out,
    attn_gain,
    conv_gain,
    conv_kernel,
    conv_scale,
):
    recs, width_t, width_d = frames.shape
    inner = w_query.shape[1]
    heads = inner // HSIZE
    shard = lax.axis_index("tm")
    local_pos = jnp.arange(width_t, dtype=jnp.int32)
    global_pos = shard * width_t + local_pos
    keep_time = keep_mask(time_starts, time_widths, global_pos)
    keep_feat = keep_mask(freq_starts, freq_widths, jnp.arange(width_d, dtype=jnp.int32))
    masked = (frames.astype(jnp.float32) * keep_time[:, :, None] * keep_feat[:, None, :]).astype(
        jnp.bfloat16
    )
    valid = (global_pos[None, :] < lengths[:, None]).astype(jnp.float32)
    normed = layer_norm(masked, attn_gain).astype(jnp.bfloat16).reshape(recs * width_t, width_d)
    query = (
        jnp.dot(normed, w_query, preferred_element_type=jnp.float32)
        .astype(jnp.bfloat16)
        .reshape(recs, width_t, inner)
    )
    keyed = (
        jnp.dot(normed, w_key, preferred_element_type=jnp.float32)
        .astype(jnp.bfloat16)
        .reshape(recs, width_t, inner)
    )
    valued = (
        jnp.dot(normed, w_value, preferred_element_type=jnp.float32)
        .astype(jnp.bfloat16)
        .reshape(recs, width_t, inner)
    )
    paired = jnp.stack((keyed, valued), axis=0)
    near = shifted(paired, "tm", 1)
    far = shifted(paired, "tm", 2)
    key_win = jnp.concatenate([far[0], near[0], keyed], axis=1)
    value_win = jnp.concatenate([far[1], near[1], valued], axis=1)
    key_pos = (shard - 2) * width_t + jnp.arange(3 * width_t, dtype=jnp.int32)
    scale = 1.0 / jnp.sqrt(jnp.float32(HSIZE))

    def attend(items):
        rows, keys_r, values_r, length = items
        rows = rows.reshape(width_t, heads, HSIZE)
        keys_r = keys_r.reshape(3 * width_t, heads, HSIZE)
        values_r = values_r.reshape(3 * width_t, heads, HSIZE)
        score = jnp.einsum("qhe,khe->hqk", rows, keys_r, preferred_element_type=jnp.float32) * scale
        allowed = (key_pos[None, :] >= 0) & (
            (key_pos[None, :] < length) | (key_pos[None, :] == global_pos[:, None])
        )
        score = jnp.where(allowed[None, :, :], score, -1e30)
        top = jnp.max(score, axis=-1, keepdims=True)
        weights = jnp.exp(score - top)
        probs = (weights / jnp.sum(weights, axis=-1, keepdims=True)).astype(jnp.bfloat16)
        context = jnp.einsum("hqk,khe->qhe", probs, values_r, preferred_element_type=jnp.float32)
        return context.reshape(width_t, inner).astype(jnp.bfloat16)

    items = (query, key_win, value_win, lengths)
    context = lax.map(attend, items)
    mixed = jnp.dot(
        context.reshape(recs * width_t, inner), w_out, preferred_element_type=jnp.float32
    ).reshape(recs, width_t, width_d)
    attended = ((masked.astype(jnp.float32) + mixed) * valid[:, :, None]).astype(jnp.bfloat16)
    conv_in = layer_norm(attended, conv_gain).astype(jnp.bfloat16)
    reach = (conv_kernel.shape[0] - 1) // 2
    padded = padded_2(conv_in, (("tm", 1),), reach).astype(jnp.float32)
    depth = jnp.zeros((recs, width_t, width_d), jnp.float32)
    for step in range(conv_kernel.shape[0]):
        depth = depth + conv_kernel[step][None, None, :] * padded[:, step : step + width_t, :]
    result = (attended.astype(jnp.float32) + conv_scale * depth * jax.nn.sigmoid(depth)) * valid[
        :, :, None
    ]
    return result.astype(jnp.bfloat16)


def solution(mesh):
    placed = (
        P("rec", "tm", None),
        P("rec", None),
        P("rec", None),
        P("rec", None),
        P("rec", None),
        P("rec"),
        P(),
        P(),
        P(),
        P(),
        P(),
        P(),
        P(),
        P(),
    )
    return jax.shard_map(
        body, mesh=mesh, in_specs=placed, out_specs=P("rec", "tm", None), check_vma=False
    )
```

profile of v0, /device:TPU:6, one launch (start us, length us, event | category | flops | bytes accessed | tf_op | source)
XLA Modules:
  0.0 145.5 jit_solution(13514771158302357010)
XLA Ops:
  0.0 0.9 add.149
  0.9 0.8 and_reduce_fusion
  1.7 0.7 add.150
  2.4 0.8 fusion.63
  3.3 1.9 %convert_reduce_fusion.1 = f32[3,128]{1,0:T(4,128)S(1)} fusion(f32[3,1536]{1,0:T(4,128)S(1)} %convert_subtract_fusion.2, f32[3,128]{1,0:T(4,128)S(1)} %convert_subtract_fusion.3, bf16[3,128,1536]{2,1,0:T(8,128)(2,1)} %param.16), kind=kLoop, calls=%fused_computation.29 | loop fusion | flops 3538560 | bytes 1201152 | tf_op jit(solution)/shard_map/reduce_sum | solution.py:41
  5.1 1.9 %fusion.26 = f32[3,128]{1,0:T(4,128)S(1)} fusion(f32[3,128]{1,0:T(4,128)S(1)} %broadcast_multiply_fusion.1, f32[3,1536]{1,0:T(4,128)S(1)} %convert_subtract_fusion.2, f32[3,128]{1,0:T(4,128)S(1)} %convert_subtract_fusion.3, bf16[3,128,1536]{2,1,0:T(8,128)(2,1)} %param.16), kind=kLoop, calls=%fused_computation.39 | loop fusion | flops 4718208 | bytes 1202688 | tf_op jit(solution)/shard_map/reduce_sum | solution.py:42
  7.1 0.6 fusion.28
  7.7 0.0 copy-start.4
  7.7 1.1 convolution_convert_fusion.2
  8.8 1.1 copy.25
  9.9 3.1 %convolution_convert_fusion.1 = bf16[384,768]{1,0:T(8,128)(2,1)S(1)} fusion(bf16[384,1536]{1,0:T(8,128)(2,1)} %bitcast.62, bf16[1536,768]{1,0:T(8,128)(2,1)} %param.24), kind=kOutput, calls=%fused_computation.111 | convolution fusion | flops 906264576 | bytes 4128768 | tf_op jit(solution)/shard_map/dot_general | solution.py:86
  13.0 0.3 copy.26
  13.4 2.2 %pad_maximum_fusion.2 = bf16[2,3,128,768]{2,3,1,0:T(8,128)(2,1)} fusion(bf16[1,3,128,768]{2,3,1,0:T(8,128)(2,1)S(1)} %copy.26, bf16[1,3,128,768]{2,3,1,0:T(8,128)(2,1)} %copy.25), kind=kLoop, calls=%fused_computation.113 | loop fusion | flops 589824 | bytes 2359296 | tf_op jit(solution)/shard_map/stack | solution.py:90
  15.5 3.8 %collective-permute-start = (bf16[2,3,128,768]{2,3,1,0:T(8,128)(2,1)}, bf16[2,3,128,768]{2,3,1,0:T(8,128)(2,1)}, u32[]{:S(2)}, u32[]{:S(2)}) collective-permute-start(bf16[2,3,128,768]{2,3,1,0:T(8,128)(2,1)} %pad_maximum_fusion.2), channel_id=1, source_target_pairs={{0,8},{4,12},{8,16},{12,20},{16,24},{20,28},{24,32},{28,36},{32,40... | collective-permute-start | bytes 3538952 | tf_op jit(solution)/shard_map/ppermute | solution.py:12
  19.4 5.1 %collective-permute-start.1 = (bf16[2,3,128,768]{2,3,1,0:T(8,128)(2,1)}, bf16[2,3,128,768]{2,3,1,0:T(8,128)(2,1)}, u32[]{:S(2)}, u32[]{:S(2)}) collective-permute-start(bf16[2,3,128,768]{2,3,1,0:T(8,128)(2,1)} %pad_maximum_fusion.2), channel_id=1, source_target_pairs={{0,4},{4,8},{8,12},{12,16},{16,20},{20,24},{24,28},{28,32},{32,36}... | collective-permute-start | bytes 3538952 | tf_op jit(solution)/shard_map/ppermute | solution.py:12
  24.5 1.4 copy.27
  25.9 1.4 copy.28
  27.2 2.2 %slice_reduce_fusion.29 = (f32[1536]{0:T(1024)S(1)}, f32[1536]{0:T(1024)}, f32[1536]{0:T(1024)}, f32[1536]{0:T(1024)}, f32[1536]{0:T(1024)}, /*index=5*/f32[1536...) fusion(f32[31,1536]{1,0:T(8,128)} %param.28), kind=kLoop, calls=%fused_computation.152 | loop fusion | bytes 147456 | tf_op jit(solution)/shard_map/slice | solution.py:125
  29.4 0.7 compare_convert_fusion
  30.2 3.9 %convolution_convert_fusion = bf16[384,768]{1,0:T(8,128)(2,1)} fusion(bf16[384,1536]{1,0:T(8,128)(2,1)} %bitcast.63, bf16[1536,768]{1,0:T(8,128)(2,1)} %param.22), kind=kOutput, calls=%fused_computation.110 | convolution fusion | flops 906264576 | bytes 4128768 | tf_op jit(solution)/shard_map/dot_general | solution.py:76
  34.1 15.7 %collective-permute-done = bf16[2,3,128,768]{2,3,1,0:T(8,128)(2,1)} collective-permute-done((bf16[2,3,128,768]{2,3,1,0:T(8,128)(2,1)}, bf16[2,3,128,768]{2,3,1,0:T(8,128)(2,1)}, u32[]{:S(2)}, u32[]{:S(2)}) %collective-permute-start) | collective-permute-done | bytes 1179680 | tf_op jit(solution)/shard_map/ppermute | solution.py:12
  49.8 1.3 slice_bitcast_fusion.1
  51.2 26.6 %collective-permute-done.1 = bf16[2,3,128,768]{2,3,1,0:T(8,128)(2,1)} collective-permute-done((bf16[2,3,128,768]{2,3,1,0:T(8,128)(2,1)}, bf16[2,3,128,768]{2,3,1,0:T(8,128)(2,1)}, u32[]{:S(2)}, u32[]{:S(2)}) %collective-permute-start.1) | collective-permute-done | bytes 1179680 | tf_op jit(solution)/shard_map/ppermute | solution.py:12
  77.7 1.3 slice_bitcast_fusion
  79.1 2.1 %pad_maximum_fusion = (bf16[3,384,768]{1,2,0:T(8,128)(2,1)}, bf16[3,384,768]{1,2,0:T(8,128)(2,1)}) fusion(bf16[3,128,768]{1,2,0:T(8,128)(2,1)S(1)} %copy.27, bf16[3,128,768]{1,2,0:T(8,128)(2,1)S(1)} %get-tuple-element.143, bf16[3,128,768]{1,2,0:T(8,128)(2,1)S(1)} %get-tuple-element.141, bf16[3,128,768]{1,2,0:T(8,128)(2,1)S(1)} %copy.28, ...), kind=kLoop, calls=%fused_computation.107 | loop fusion | flops 10616832 | bytes 7077888 | tf_op jit(solution)/shard_map/concatenate | solution.py:94
  81.1 35.6 %while.11 = (s32[]{:T(128)}, bf16[3,128,768]{1,2,0:T(8,128)(2,1)}, bf16[3,384,768]{1,2,0:T(8,128)(2,1)}, s32[3]{0:T(128)}, bf16[3,128,768]{2,1,0:T(8,128)(2,1)},...) while((s32[]{:T(128)}, bf16[3,128,768]{1,2,0:T(8,128)(2,1)}, ...), condition=%wide.region_7.8_spmd.clone, body=%wide.region_4.7_spmd.clone.sunk | while | flops 154781696 | bytes 9947265 | solution.py:115
  81.1 1.2 dynamic_slice.27
  82.4 0.7 fusion.85
  83.1 0.1 or_and_fusion.2
  83.2 2.2 %constant_dynamic-slice_fusion.5 = (bf16[1,384,768]{1,2,0:T(8,128)(2,1)}, bf16[1,384,768]{1,2,0:T(8,128)(2,1)S(1)}) fusion(bf16[3,384,768]{1,2,0:T(8,128)(2,1)} %get-tuple-element.232, s32[]{:T(128)} %get-tuple-element.218, bf16[3,384,768]{1,2,0:T(8,128)(2,1)} %get-tuple-element.229), kind=kLoop, calls=%fused_computation.18.clone.1 | loop fusion | bytes 2359300 | tf_op jit(solution)/shard_map/while/body/jit(dynamic_index_in_dim)/dynamic_slice | solution.py:115
  85.4 0.9 constant_dynamic-slice_fusion.6
  86.3 0.2 copy.34
  86.5 3.5 %fusion.86 = (f32[12,128]{1,0:T(8,128)S(1)}, f32[12,128,384]{2,1,0:T(8,128)}) fusion(pred[128,384]{1,0:T(8,128)(4,1)S(1)} %or_and_fusion.2, bf16[128,12,64]{0,2,1:T(8,128)(2,1)S(1)} %bitcast.54, bf16[384,12,64]{0,2,1:T(8,128)(2,1)} %bitcast.53), kind=kOutput, calls=%fused_computation.162.clone.1 | convolution fusion | flops 77857152 | bytes 3201024 | tf_op jit(solution)/shard_map/while/body/eval_jaxpr/sub | solution.py:109
  89.9 2.4 %fusion.87 = bf16[12,64,128]{2,1,0:T(8,128)(2,1)S(1)} fusion(bf16[384,12,64]{0,2,1:T(8,128)(2,1)S(1)} %bitcast.52, f32[12,128,384]{2,1,0:T(8,128)} %get-tuple-element.207, f32[12,128]{1,0:T(8,128)S(1)} %get-tuple-element.208), kind=kOutput, calls=%fused_computation.11.clone.1 | convolution fusion | flops 76775424 | bytes 3151872 | tf_op jit(solution)/shard_map/while/body/eval_jaxpr/hqk,khe->qhe/dot_general | solution.py:111
  92.3 0.7 constant_dynamic-update-slice_fusion.2
  93.0 1.2 dynamic_slice.27
  94.3 0.7 fusion.85
  95.0 0.1 or_and_fusion.2
  95.1 2.2 %constant_dynamic-slice_fusion.5 = (bf16[1,384,768]{1,2,0:T(8,128)(2,1)}, bf16[1,384,768]{1,2,0:T(8,128)(2,1)S(1)}) fusion(bf16[3,384,768]{1,2,0:T(8,128)(2,1)} %get-tuple-element.232, s32[]{:T(128)} %get-tuple-element.218, bf16[3,384,768]{1,2,0:T(8,128)(2,1)} %get-tuple-element.229), kind=kLoop, calls=%fused_computation.18.clone.1 | loop fusion | bytes 2359300 | tf_op jit(solution)/shard_map/while/body/jit(dynamic_index_in_dim)/dynamic_slice | solution.py:115
  97.3 0.9 constant_dynamic-slice_fusion.6
  98.2 0.2 copy.34
  98.4 3.5 %fusion.86 = (f32[12,128]{1,0:T(8,128)S(1)}, f32[12,128,384]{2,1,0:T(8,128)}) fusion(pred[128,384]{1,0:T(8,128)(4,1)S(1)} %or_and_fusion.2, bf16[128,12,64]{0,2,1:T(8,128)(2,1)S(1)} %bitcast.54, bf16[384,12,64]{0,2,1:T(8,128)(2,1)} %bitcast.53), kind=kOutput, calls=%fused_computation.162.clone.1 | convolution fusion | flops 77857152 | bytes 3201024 | tf_op jit(solution)/shard_map/while/body/eval_jaxpr/sub | solution.py:109
  101.8 2.4 %fusion.87 = bf16[12,64,128]{2,1,0:T(8,128)(2,1)S(1)} fusion(bf16[384,12,64]{0,2,1:T(8,128)(2,1)S(1)} %bitcast.52, f32[12,128,384]{2,1,0:T(8,128)} %get-tuple-element.207, f32[12,128]{1,0:T(8,128)S(1)} %get-tuple-element.208), kind=kOutput, calls=%fused_computation.11.clone.1 | convolution fusion | flops 76775424 | bytes 3151872 | tf_op jit(solution)/shard_map/while/body/eval_jaxpr/hqk,khe->qhe/dot_general | solution.py:111
  104.2 0.7 constant_dynamic-update-slice_fusion.2
  104.9 1.2 dynamic_slice.27
  106.1 0.7 fusion.85
  106.8 0.1 or_and_fusion.2
  106.9 2.2 %constant_dynamic-slice_fusion.5 = (bf16[1,384,768]{1,2,0:T(8,128)(2,1)}, bf16[1,384,768]{1,2,0:T(8,128)(2,1)S(1)}) fusion(bf16[3,384,768]{1,2,0:T(8,128)(2,1)} %get-tuple-element.232, s32[]{:T(128)} %get-tuple-element.218, bf16[3,384,768]{1,2,0:T(8,128)(2,1)} %get-tuple-element.229), kind=kLoop, calls=%fused_computation.18.clone.1 | loop fusion | bytes 2359300 | tf_op jit(solution)/shard_map/while/body/jit(dynamic_index_in_dim)/dynamic_slice | solution.py:115
  109.1 0.9 constant_dynamic-slice_fusion.6
  110.1 0.2 copy.34
  110.2 3.5 %fusion.86 = (f32[12,128]{1,0:T(8,128)S(1)}, f32[12,128,384]{2,1,0:T(8,128)}) fusion(pred[128,384]{1,0:T(8,128)(4,1)S(1)} %or_and_fusion.2, bf16[128,12,64]{0,2,1:T(8,128)(2,1)S(1)} %bitcast.54, bf16[384,12,64]{0,2,1:T(8,128)(2,1)} %bitcast.53), kind=kOutput, calls=%fused_computation.162.clone.1 | convolution fusion | flops 77857152 | bytes 3201024 | tf_op jit(solution)/shard_map/while/body/eval_jaxpr/sub | solution.py:109
  113.7 2.4 %fusion.87 = bf16[12,64,128]{2,1,0:T(8,128)(2,1)S(1)} fusion(bf16[384,12,64]{0,2,1:T(8,128)(2,1)S(1)} %bitcast.52, f32[12,128,384]{2,1,0:T(8,128)} %get-tuple-element.207, f32[12,128]{1,0:T(8,128)S(1)} %get-tuple-element.208), kind=kOutput, calls=%fused_computation.11.clone.1 | convolution fusion | flops 76775424 | bytes 3151872 | tf_op jit(solution)/shard_map/while/body/eval_jaxpr/hqk,khe->qhe/dot_general | solution.py:111
  116.1 0.7 constant_dynamic-update-slice_fusion.2
  116.8 2.8 %convert_reduce_fusion = (f32[3,128]{1,0:T(4,128)S(1)}, bf16[3,128,1536]{2,1,0:T(8,128)(2,1)S(1)}) fusion(f32[3,128]{1,0:T(4,128)S(1)} %compare_convert_fusion, bf16[3,128,768]{1,2,0:T(8,128)(2,1)} %get-tuple-element.47, bf16[768,1536]{1,0:T(8,128)(2,1)S(1)} %copy-done, f32[3,1536]{1,0:T(4,128)S(1)} %copy-done.6, f32[3,128]{1,0:T(4,128)S(1)} %convert_subtract_fusion.3, ...), kind=kOutput, calls=%fused_computation.26 | convolution fusion | flops 911867520 | bytes 5331456 | tf_op jit(solution)/shard_map/dot_general | solution.py:116
  119.6 0.4 fusion.23
  120.1 0.4 fusion.25
  120.6 1.9 %collective-permute-start.2 = (bf16[3,15,1536]{2,1,0:T(8,128)(2,1)S(1)}, bf16[3,15,1536]{2,1,0:T(8,128)(2,1)S(1)}, u32[]{:S(2)}, u32[]{:S(2)}) collective-permute-start(bf16[3,15,1536]{2,1,0:T(8,128)(2,1)S(1)} %get-tuple-element.138), channel_id=1, source_target_pairs={{0,4},{4,8},{8,12},{12,16},{16,20},{20,24},{24,28},{28,32},{32,36}... | collective-permute-start | bytes 414728 | tf_op jit(solution)/shard_map/ppermute | solution.py:23
  122.6 0.0 copy-start.21
  122.6 8.7 %collective-permute-start.3 = (bf16[3,15,1536]{2,1,0:T(8,128)(2,1)S(1)}, bf16[3,15,1536]{2,1,0:T(8,128)(2,1)S(1)}, u32[]{:S(2)}, u32[]{:S(2)}) collective-permute-start(bf16[3,15,1536]{2,1,0:T(8,128)(2,1)S(1)} %get-tuple-element.139), channel_id=1, source_target_pairs={{4,0},{8,4},{12,8},{16,12},{20,16},{24,20},{28,24},{32,28},{36,32}... | collective-permute-start | bytes 414728 | tf_op jit(solution)/shard_map/ppermute | solution.py:25
  131.4 0.3 slice_reduce_fusion.30
  131.7 0.4 collective-permute-done.2
  132.1 2.2 %collective-permute-done.3 = bf16[3,15,1536]{2,1,0:T(8,128)(2,1)S(1)} collective-permute-done((bf16[3,15,1536]{2,1,0:T(8,128)(2,1)S(1)}, bf16[3,15,1536]{2,1,0:T(8,128)(2,1)S(1)}, u32[]{:S(2)}, u32[]{:S(2)}) %collective-permute-start.3) | collective-permute-done | bytes 138272 | tf_op jit(solution)/shard_map/ppermute | solution.py:25
  134.4 0.4 maximum_convert_fusion
  134.9 10.5 %fusion.30 = bf16[3,128,1536]{2,1,0:T(8,128)(2,1)} fusion(bf16[3,128,1536]{2,1,0:T(8,128)(2,1)S(1)} %get-tuple-element.145, f32[3,158,1536]{2,1,0:T(8,128)S(1)} %maximum_convert_fusion, f32[1536]{0:T(1024)S(1)} %copy-done.17, f32[1536]{0:T(1024)S(1)} %copy-done.18, f32[1536]{0:T(1024)S(1)} %get-tuple-element.86, f32[1536]{0:T(1024)S(1)} %get-tuple-element.87, ...), kind=kLoop, calls=%fused_computation.43 | loop fusion | flops 41287680 | bytes 75695616 | tf_op jit(solution)/shard_map/convert_element_type | solution.py:129
  (61 shorter events, 0.2 us)
Async XLA Ops:
  0.0 116.8 %copy-start = (bf16[768,1536]{1,0:T(8,128)(2,1)S(1)}, bf16[768,1536]{1,0:T(8,128)(2,1)}, u32[]{:S(2)}) copy-start(bf16[768,1536]{1,0:T(8,128)(2,1)} %param.25) | copy-start | bytes 7077892
  0.0 7.0 %copy-start.1 = (bf16[3,128,1536]{2,1,0:T(8,128)(2,1)S(1)}, bf16[3,128,1536]{2,1,0:T(8,128)(2,1)}, u32[]{:S(2)}) copy-start(bf16[3,128,1536]{2,1,0:T(8,128)(2,1)} %param.16) | copy-start | bytes 3538948
  0.0 7.0 %copy-start.19 = (f32[1536]{0:T(1024)S(1)}, f32[1536]{0:T(1024)}, u32[]{:S(2)}) copy-start(f32[1536]{0:T(1024)} %param.26) | copy-start | bytes 18436
  0.0 1.7 %copy-start.22 = (s32[128]{0:T(128)}, s32[128]{0:T(128)S(1)}, u32[]{:S(2)}) copy-start(s32[128]{0:T(128)S(1)} %iota_add_fusion.2) | copy-start | bytes 1540
  3.2 4.5 %copy-start.5 = (f32[3,1536]{1,0:T(4,128)}, f32[3,1536]{1,0:T(4,128)S(1)}, u32[]{:S(2)}) copy-start(f32[3,1536]{1,0:T(4,128)S(1)} %convert_subtract_fusion.2) | copy-start | bytes 55300
  3.2 4.5 %copy-start.23 = (bf16[1536,768]{1,0:T(8,128)(2,1)S(1)}, bf16[1536,768]{1,0:T(8,128)(2,1)}, u32[]{:S(2)}) copy-start(bf16[1536,768]{1,0:T(8,128)(2,1)} %param.23) | copy-start | bytes 7077892
  7.7 1.1 copy-start.4
  8.8 4.2 %copy-start.2 = (bf16[384,768]{1,0:T(8,128)(2,1)}, bf16[384,768]{1,0:T(8,128)(2,1)S(1)}, u32[]{:S(2)}) copy-start(bf16[384,768]{1,0:T(8,128)(2,1)S(1)} %convolution_convert_fusion.2) | copy-start | bytes 1769476
  13.0 11.4 %copy-start.3 = (bf16[384,768]{1,0:T(8,128)(2,1)}, bf16[384,768]{1,0:T(8,128)(2,1)S(1)}, u32[]{:S(2)}) copy-start(bf16[384,768]{1,0:T(8,128)(2,1)S(1)} %convolution_convert_fusion.1) | copy-start | bytes 1769476
  15.5 34.3 %collective-permute-start = (bf16[2,3,128,768]{2,3,1,0:T(8,128)(2,1)}, bf16[2,3,128,768]{2,3,1,0:T(8,128)(2,1)}, u32[]{:S(2)}, u32[]{:S(2)}) collective-permute-start(bf16[2,3,128,768]{2,3,1,0:T(8,128)(2,1)} %pad_maximum_fusion.2), channel_id=1, source_target_pairs={{0,8},{4,12},{8,16},{12,20},{16,24},{20,28},{24,32},{28,36},{32,40... | collective-permute-start | bytes 3538952 | tf_op jit(solution)/shard_map/ppermute | solution.py:12
  19.4 58.4 %collective-permute-start.1 = (bf16[2,3,128,768]{2,3,1,0:T(8,128)(2,1)}, bf16[2,3,128,768]{2,3,1,0:T(8,128)(2,1)}, u32[]{:S(2)}, u32[]{:S(2)}) collective-permute-start(bf16[2,3,128,768]{2,3,1,0:T(8,128)(2,1)} %pad_maximum_fusion.2), channel_id=1, source_target_pairs={{0,4},{4,8},{8,12},{12,16},{16,20},{20,24},{24,28},{28,32},{32,36}... | collective-permute-start | bytes 3538952 | tf_op jit(solution)/shard_map/ppermute | solution.py:12
  81.1 35.6 %copy-start.6 = (f32[3,1536]{1,0:T(4,128)S(1)}, f32[3,1536]{1,0:T(4,128)}, u32[]{:S(2)}) copy-start(f32[3,1536]{1,0:T(4,128)} %copy-done.5) | copy-start | bytes 55300
  116.8 3.3 %copy-start.20 = (f32[1536]{0:T(1024)S(1)}, f32[1536]{0:T(1024)}, u32[]{:S(2)}) copy-start(f32[1536]{0:T(1024)} %param.27) | copy-start | bytes 18436
  119.6 11.8 %copy-start.7 = (f32[31,1536]{1,0:T(8,128)S(1)}, f32[31,1536]{1,0:T(8,128)}, u32[]{:S(2)}) copy-start(f32[31,1536]{1,0:T(8,128)} %param.28) | copy-start | bytes 571396
  120.6 11.6 %collective-permute-start.2 = (bf16[3,15,1536]{2,1,0:T(8,128)(2,1)S(1)}, bf16[3,15,1536]{2,1,0:T(8,128)(2,1)S(1)}, u32[]{:S(2)}, u32[]{:S(2)}) collective-permute-start(bf16[3,15,1536]{2,1,0:T(8,128)(2,1)S(1)} %get-tuple-element.138), channel_id=1, source_target_pairs={{0,4},{4,8},{8,12},{12,16},{16,20},{20,24},{24,28},{28,32},{32,36}... | collective-permute-start | bytes 414728 | tf_op jit(solution)/shard_map/ppermute | solution.py:23
  122.5 12.3 %copy-start.8 = (f32[1536]{0:T(1024)S(1)}, f32[1536]{0:T(1024)}, u32[]{:S(2)}) copy-start(f32[1536]{0:T(1024)} %get-tuple-element.105) | copy-start | bytes 18436
  122.5 12.3 %copy-start.9 = (f32[1536]{0:T(1024)S(1)}, f32[1536]{0:T(1024)}, u32[]{:S(2)}) copy-start(f32[1536]{0:T(1024)} %get-tuple-element.106) | copy-start | bytes 18436
  122.5 12.3 %copy-start.10 = (f32[1536]{0:T(1024)S(1)}, f32[1536]{0:T(1024)}, u32[]{:S(2)}) copy-start(f32[1536]{0:T(1024)} %get-tuple-element.107) | copy-start | bytes 18436
  122.5 12.3 %copy-start.11 = (f32[1536]{0:T(1024)S(1)}, f32[1536]{0:T(1024)}, u32[]{:S(2)}) copy-start(f32[1536]{0:T(1024)} %get-tuple-element.108) | copy-start | bytes 18436
  122.5 12.3 %copy-start.12 = (f32[1536]{0:T(1024)S(1)}, f32[1536]{0:T(1024)}, u32[]{:S(2)}) copy-start(f32[1536]{0:T(1024)} %get-tuple-element.109) | copy-start | bytes 18436
  122.6 12.3 %copy-start.13 = (f32[1536]{0:T(1024)S(1)}, f32[1536]{0:T(1024)}, u32[]{:S(2)}) copy-start(f32[1536]{0:T(1024)} %get-tuple-element.110) | copy-start | bytes 18436
  122.6 12.3 %copy-start.14 = (f32[1536]{0:T(1024)S(1)}, f32[1536]{0:T(1024)}, u32[]{:S(2)}) copy-start(f32[1536]{0:T(1024)} %get-tuple-element.111) | copy-start | bytes 18436
  122.6 12.3 %copy-start.15 = (f32[1536]{0:T(1024)S(1)}, f32[1536]{0:T(1024)}, u32[]{:S(2)}) copy-start(f32[1536]{0:T(1024)} %get-tuple-element.112) | copy-start | bytes 18436
  122.6 12.3 %copy-start.16 = (f32[1536]{0:T(1024)S(1)}, f32[1536]{0:T(1024)}, u32[]{:S(2)}) copy-start(f32[1536]{0:T(1024)} %get-tuple-element.113) | copy-start | bytes 18436
  122.6 12.3 %copy-start.17 = (f32[1536]{0:T(1024)S(1)}, f32[1536]{0:T(1024)}, u32[]{:S(2)}) copy-start(f32[1536]{0:T(1024)} %get-tuple-element.114) | copy-start | bytes 18436
  122.6 12.3 %copy-start.18 = (f32[1536]{0:T(1024)S(1)}, f32[1536]{0:T(1024)}, u32[]{:S(2)}) copy-start(f32[1536]{0:T(1024)} %get-tuple-element.115) | copy-start | bytes 18436
  122.6 12.3 %copy-start.21 = (f32[1536]{0:T(1024)S(1)}, f32[1536]{0:T(1024)}, u32[]{:S(2)}) copy-start(f32[1536]{0:T(1024)} %param.29) | copy-start | bytes 18436
  122.6 11.7 %collective-permute-start.3 = (bf16[3,15,1536]{2,1,0:T(8,128)(2,1)S(1)}, bf16[3,15,1536]{2,1,0:T(8,128)(2,1)S(1)}, u32[]{:S(2)}, u32[]{:S(2)}) collective-permute-start(bf16[3,15,1536]{2,1,0:T(8,128)(2,1)S(1)} %get-tuple-element.139), channel_id=1, source_target_pairs={{4,0},{8,4},{12,8},{16,12},{20,16},{24,20},{28,24},{32,28},{36,32}... | collective-permute-start | bytes 414728 | tf_op jit(solution)/shard_map/ppermute | solution.py:25
where the time goes:
time: 147 us; the launch traced here: 145 us
  waiting for transfers between devices  44.9 us (31%)
  matrix products  28.4 us (19%)
  other arithmetic  26.8 us (18%)
  local copies, waits for them, and re-layouts  25.1 us (17%)
  starting transfers between devices  19.6 us (13%)
    ppermute x2, waiting for transfers between devices, shifted(): return lax.ppermute(block, axis, route)  42.3 us
    dynamic_slice x12, local copies, waits for them, and re-layouts, body(): context = lax.map(attend, items)  13.6 us
    convert_element_type x1, other arithmetic, body(): return result.astype(jnp.bfloat16)  10.5 us
    sub x3, matrix products, attend(): weights = jnp.exp(score - top)  10.4 us
    ppermute x2, starting transfers between devices, shifted(): return lax.ppermute(block, axis, route)  8.92 us
    ppermute x1, starting transfers between devices, padded_2(): lax.ppermute(head, axis, [((i + 1) % count, i) for i in range(ends)])  8.75 us
    dot_general x3, matrix products, attend(): jnp.einsum('hqk,khe->qhe', probs, values_r, preferred_element_type=jnp.fl...  7.13 us
    dot_general x1, matrix products, body(): jnp.dot(normed, w_query, preferred_element_type=jnp.float32)  3.94 us
  transfers between devices with their start and end apart: 4, of which 4 were waited for; matrix products, arithmetic and copies ran while one was open for 8% of the time, Pallas kernels for 0%

commit v1 on v0

v1 whole, which is shorter than its diff:
```python
import functools

import jax
import jax.numpy as jnp
from jax import lax
from jax.experimental import pallas as pl
from jax.experimental.pallas import tpu as pltpu
from jax.sharding import PartitionSpec as P

MESH = pl.DeviceIdType.MESH
HSIZE = 64
GROUP = 256
PAD = 16
LANES = 128
AHEAD = 2
LAG = 5


def layer_norm(values, gain):
    center = jnp.mean(values, axis=-1, keepdims=True)
    moved = values - center
    spread = jnp.mean(moved * moved, axis=-1, keepdims=True)
    return moved * lax.rsqrt(spread + 1e-05) * gain


def kernel(
    n,
    time_starts,
    time_widths,
    freq_starts,
    freq_widths,
    lengths,
    frames,
    w_query,
    w_key,
    w_value,
    w_out,
    attn_gain,
    conv_gain,
    conv_kernel,
    conv_scale,
    out,
    masked,
    wq,
    wk,
    wv,
    wo,
    normed,
    query,
    window,
    context,
    attended,
    padded,
    result,
    gains,
    load_sem,
    out_sem,
    z_send,
    z_recv,
    y_send,
    y_recv,
    halo_send,
    halo_recv,
):
    recs, rows, width = masked.shape
    groups = window.shape[0] // recs
    pieces = recs * groups
    wide = width // groups
    me = lax.axis_index("tm")
    odd = lax.rem(me, 2)
    ahead = lax.rem(me + 2, n)
    behind = lax.rem(me + n - 2, n)
    mate = me + 1 - 2 * odd
    other = lax.rem(me + n - 1 + 2 * odd, n)
    after = lax.rem(me + 1, n)
    before = lax.rem(me + n - 1, n)

    loads = []
    for k, (src, dst) in enumerate(
        ((frames, masked), (w_key, wk), (w_value, wv), (w_query, wq), (w_out, wo))
    ):
        copy = pltpu.make_async_copy(src, dst, load_sem.at[k])
        copy.start()
        loads.append(copy)

    barrier = pltpu.get_barrier_semaphore()
    for peer in (behind, mate, other):
        pl.semaphore_signal(barrier, inc=1, device_id={"tm": peer}, device_id_type=MESH)

    local = lax.broadcasted_iota(jnp.int32, (rows, 1), 0)
    place = me * rows + local
    feature = lax.broadcasted_iota(jnp.int32, (1, width), 1)

    def cut(starts, widths, r, places):
        keep = jnp.ones(places.shape, jnp.float32)
        for m in range(starts.shape[0]):
            first = starts[m, r]
            inside = (places >= first) & (places < first + widths[m, r])
            keep = jnp.where(inside, 0.0, keep)
        return keep

    def prepare(r):
        values = masked[r].astype(jnp.float32)
        values = values * cut(time_starts, time_widths, r, place)
        values = values * cut(freq_starts, freq_widths, r, feature)
        masked[r] = values.astype(jnp.bfloat16)
        normed[r] = layer_norm(values, gains[0]).astype(jnp.bfloat16)

    for c in range(width // LANES):
        cols = pl.ds(c * LANES, LANES)
        gains[0, :, cols] = attn_gain[pl.ds(c, 1), :]
        gains[1, :, cols] = conv_gain[pl.ds(c, 1), :]

    def z_copy(k):
        return pltpu.make_async_remote_copy(
            src_ref=window.at[k, pl.ds(2 * rows, rows)],
            dst_ref=window.at[k, pl.ds(0, rows)],
            send_sem=z_send.at[k],
            recv_sem=z_recv.at[k],
            device_id={"tm": ahead},
            device_id_type=MESH,
        )

    def y_copy(k, first):
        return pltpu.make_async_remote_copy(
            src_ref=window.at[k, pl.ds(first, rows)],
            dst_ref=window.at[k, pl.ds(rows, rows)],
            send_sem=y_send.at[k],
            recv_sem=y_recv.at[k],
            device_id={"tm": mate},
            device_id_type=MESH,
        )

    def project(r):
        own = normed[r]
        for g in range(groups):
            cols = pl.ds(g * GROUP, GROUP)
            k = r * groups + g
            window[k, pl.ds(2 * rows, rows), pl.ds(0, GROUP)] = jnp.dot(
                own, wk[:, cols], preferred_element_type=jnp.float32
            ).astype(jnp.bfloat16)
            window[k, pl.ds(2 * rows, rows), pl.ds(GROUP, GROUP)] = jnp.dot(
                own, wv[:, cols], preferred_element_type=jnp.float32
            ).astype(jnp.bfloat16)

    loads[0].wait()
    prepare(0)
    loads[1].wait()
    loads[2].wait()
    project(0)
    pl.semaphore_wait(barrier, 3)
    for k in range(AHEAD):
        z_copy(k).start()

    @pl.when(odd == 0)
    def _():
        y_copy(0, 2 * rows).start()

    def more(r, _):
        prepare(r)
        project(r)
        return 0

    lax.fori_loop(1, recs, more, 0)

    loads[3].wait()

    def ask(r, _):
        own = normed[r]
        for g in range(groups):
            cols = pl.ds(g * GROUP, GROUP)
            asked = jnp.dot(own, wq[:, cols], preferred_element_type=jnp.float32)
            query[r * groups + g] = asked.astype(jnp.bfloat16) * jnp.bfloat16(HSIZE**-0.5)
        return 0

    lax.fori_loop(0, recs, ask, 0)
    loads[4].wait()

    heads = GROUP // HSIZE
    head_of = lax.broadcasted_iota(jnp.int32, (1, GROUP), 1) // HSIZE

    def attend(k):
        r = k // groups
        length = lengths[r]
        keys = window[k, :, pl.ds(0, GROUP)]
        values = window[k, :, pl.ds(GROUP, GROUP)]
        asked = query[k]
        stacked = jnp.concatenate(
            [jnp.where(head_of == h, asked, jnp.zeros_like(asked)) for h in range(heads)], axis=0
        )
        score = lax.dot_general(
            stacked, keys, (((1,), (1,)), ((), ())), preferred_element_type=jnp.float32
        )
        key_pos = (me - 2) * rows + lax.broadcasted_iota(jnp.int32, (rows, 3 * rows), 1)
        allowed = (key_pos >= 0) & ((key_pos < length) | (key_pos == place))
        allowed = jnp.concatenate([allowed] * heads, axis=0)
        score = jnp.where(allowed, score, -1e30)
        top = jnp.max(score, axis=-1, keepdims=True)
        weights = jnp.exp(score - top)
        total = jnp.sum(weights, axis=-1, keepdims=True)
        mixed = jnp.dot(weights.astype(jnp.bfloat16), values, preferred_element_type=jnp.float32)
        mixed = mixed / total
        own = mixed[0:rows]
        for h in range(1, heads):
            own = jnp.where(head_of == h, mixed[h * rows : (h + 1) * rows], own)
        g = lax.rem(k, groups)
        context[r, :, pl.ds(pl.multiple_of(g * GROUP, GROUP), GROUP)] = own.astype(jnp.bfloat16)

    def halo(r, side):
        target = after if side else before
        source = rows if side else PAD
        dest = 0 if side else rows + PAD
        return pltpu.make_async_remote_copy(
            src_ref=padded.at[r, pl.ds(source, PAD)],
            dst_ref=padded.at[r, pl.ds(dest, PAD)],
            send_sem=halo_send.at[r, side],
            recv_sem=halo_recv.at[r, side],
            device_id={"tm": target},
            device_id_type=MESH,
        )

    def finish(r):
        mixed = jnp.dot(context[r], wo[...], preferred_element_type=jnp.float32)
        valid = (place < lengths[r]).astype(jnp.float32)
        held = ((masked[r].astype(jnp.float32) + mixed) * valid).astype(jnp.bfloat16)
        attended[r] = held
        padded[r, pl.ds(PAD, rows)] = layer_norm(
            held.astype(jnp.float32), gains[1]
        ).astype(jnp.bfloat16)
        halo(r, 0).start()
        halo(r, 1).start()

    lead = jnp.where(me > 0, 1.0, 0.0)
    tail = jnp.where(me < n - 1, 1.0, 0.0)
    strips = rows // 8

    def convolve(r, g):
        valid = (place < lengths[r]).astype(jnp.float32)

        def tile(c, _):
            cols = pl.ds(pl.multiple_of(g * wide + c * 128, 128), 128)
            cells = padded[r, :, cols].astype(jnp.float32)
            cells = jnp.concatenate(
                [cells[0:PAD] * lead, cells[PAD : PAD + rows], cells[PAD + rows :] * tail], axis=0
            )
            taps = conv_kernel[:, cols]
            depth = jnp.zeros((rows, 128), jnp.float32)
            for b in range(8):
                part = None
                for a in range(4):
                    j = 8 * a + b
                    if j == 0:
                        continue
                    term = taps[j - 1 : j] * cells[8 * a : 8 * a + rows + 8]
                    part = term if part is None else part + term
                depth = depth + part[b : b + rows]
            held = attended[r, :, cols].astype(jnp.float32)
            gate = depth / (1.0 + jnp.exp(-depth))
            done = (held + conv_scale[pl.ds(g * (wide // LANES) + c, 1), :] * gate) * valid
            result[r, :, cols] = done.astype(jnp.bfloat16)
            return 0

        lax.fori_loop(0, wide // 128, tile, 0)

    def write(r):
        return pltpu.make_async_copy(result.at[r], out.at[r], out_sem.at[r])

    def conv_piece(q):
        r = q // groups
        g = lax.rem(q, groups)

        @pl.when(g == 0)
        def _():
            halo(r, 0).wait_recv()
            halo(r, 1).wait_recv()

        convolve(r, g)

        @pl.when(g == groups - 1)
        def _():
            write(r).start()

    def step(k, _):
        @pl.when(k < pieces)
        def _():
            z_copy(k).wait_recv()

            @pl.when(k + AHEAD < pieces)
            def _():
                z_copy(k + AHEAD).start()

            @pl.when(odd == 1)
            def _():
                y_copy(k, 0).start()

            @pl.when((odd == 0) & (k + 1 < pieces))
            def _():
                y_copy(k + 1, 2 * rows).start()

        @pl.when(k > 0)
        def _():
            p = k - 1
            y_copy(p, 0).wait_recv()
            attend(p)

            @pl.when(lax.rem(p, groups) == groups - 1)
            def _():
                finish(p // groups)

            @pl.when(p >= LAG)
            def _():
                conv_piece(p - LAG)

        return 0

    lax.fori_loop(0, pieces + 1, step, 0)

    def rest(q, _):
        conv_piece(q)
        return 0

    lax.fori_loop(pieces - LAG, pieces, rest, 0)

    def settle(k, _):
        z_copy(k).wait_send()
        y_copy(k, 0).wait_send()
        return 0

    lax.fori_loop(0, pieces, settle, 0)
    for r in range(recs):
        halo(r, 0).wait_send()
        halo(r, 1).wait_send()
        write(r).wait()


def body(
    frames,
    time_starts,
    time_widths,
    freq_starts,
    freq_widths,
    lengths,
    w_query,
    w_key,
    w_value,
    w_out,
    attn_gain,
    conv_gain,
    conv_kernel,
    conv_scale,
):
    n = lax.axis_size("tm")
    recs, rows, width = frames.shape
    inner = w_query.shape[1]
    groups = inner // GROUP
    pieces = recs * groups
    smem = pl.BlockSpec(memory_space=pltpu.SMEM)
    vmem = pl.BlockSpec(memory_space=pltpu.VMEM)
    hbm = pl.BlockSpec(memory_space=pl.ANY)
    dma = pltpu.SemaphoreType.DMA
    return pl.pallas_call(
        functools.partial(kernel, n),
        out_shape=jax.ShapeDtypeStruct((recs, rows, width), jnp.bfloat16),
        in_specs=[smem] * 5 + [hbm] * 5 + [vmem] * 4,
        out_specs=hbm,
        scratch_shapes=[
            pltpu.VMEM((recs, rows, width), jnp.bfloat16),
            pltpu.VMEM((width, inner), jnp.bfloat16),
            pltpu.VMEM((width, inner), jnp.bfloat16),
            pltpu.VMEM((width, inner), jnp.bfloat16),
            pltpu.VMEM((inner, width), jnp.bfloat16),
            pltpu.VMEM((recs, rows, width), jnp.bfloat16),
            pltpu.VMEM((pieces, rows, GROUP), jnp.bfloat16),
            pltpu.VMEM((pieces, 3 * rows, 2 * GROUP), jnp.bfloat16),
            pltpu.VMEM((recs, rows, inner), jnp.bfloat16),
            pltpu.VMEM((recs, rows, width), jnp.bfloat16),
            pltpu.VMEM((recs, rows + 2 * PAD, width), jnp.bfloat16),
            pltpu.VMEM((recs, rows, width), jnp.bfloat16),
            pltpu.VMEM((2, 1, width), jnp.float32),
            dma((5,)),
            dma((recs,)),
            dma((pieces,)),
            dma((pieces,)),
            dma((pieces,)),
            dma((pieces,)),
            dma((recs, 2)),
            dma((recs, 2)),
        ],
        compiler_params=pltpu.CompilerParams(
            collective_id=0, has_side_effects=True, vmem_limit_bytes=56 * 1024 * 1024
        ),
        name="layer",
    )(
        time_starts.T,
        time_widths.T,
        freq_starts.T,
        freq_widths.T,
        lengths,
        frames,
        w_query,
        w_key,
        w_value,
        w_out,
        attn_gain.reshape(width // LANES, LANES),
        conv_gain.reshape(width // LANES, LANES),
        conv_kernel,
        conv_scale.reshape(width // LANES, LANES),
    )


def solution(mesh):
    placed = (
        P("rec", "tm", None),
        P("rec", None),
        P("rec", None),
        P("rec", None),
        P("rec", None),
        P("rec"),
        P(),
        P(),
        P(),
        P(),
        P(),
        P(),
        P(),
        P(),
    )
    return jax.shard_map(
        body, mesh=mesh, in_specs=placed, out_specs=P("rec", "tm", None), check_vma=False
    )
```

time: 147 us -> 60.6 us (0.41)
  the two profiles are of different devices: /device:TPU:6 before, /device:TPU:16 now
where the time goes in v1:
time: 60.6 us; the launch traced here: 60.5 us
  Pallas kernels  58.2 us (96%)
  local copies, waits for them, and re-layouts  2.36 us (4%)
    pallas_call x1, Pallas kernels, body(): pl.pallas_call(functools.partial(kernel, n), out_shape=jax.ShapeDtypeStru...  58.2 us
    unnamed x1, local copies, waits for them, and re-layouts  2.36 us

profile of v1, /device:TPU:16, one launch (start us, length us, event | category | flops | bytes accessed | tf_op | source)
XLA Modules:
  0.0 60.5 jit_solution(867293742395594279)
XLA Ops:
  0.0 58.2 %layer.1 = bf16[3,128,1536]{2,1,0:T(8,128)(2,1)} custom-call(s32[2,3]{1,0:T(2,128)} %bitcast.10, s32[2,3]{1,0:T(2,128)} %bitcast.11, s32[2,3]{1,0:T(2,128)} %bitcast.12, s32[2,3]{1,0:T(2,128)} %bitcast.13, s32[3]{0:T(128)} %lengths.1, bf16[3,128,1536]{2,1,0:T(8,128)(2,1)} %frames.1, bf16[1536,768]{1,0:T(8,128)(2,1)} %w_query.1, bf16[1536,768]{1,0:T(8,128)(2,1)} %w_key.1, ...), custom_call_target="tpu_custom_call" | custom-call | tf_op jit(solution)/shard_map/layer/pallas_call | solution.py:361
  58.2 2.4 %copy.16 = bf16[3,128,1536]{2,1,0:T(8,128)(2,1)} copy(bf16[3,128,1536]{2,1,0:T(8,128)(2,1)} %layer.1) | data formatting | bytes 2359296

commit v2 on v1

--- a/solution.py
+++ b/solution.py
@@ -12,7 +12,7 @@
 GROUP = 256
 PAD = 16
 LANES = 128
-AHEAD = 2
+AHEAD = 3
 LAG = 5
 
 
@@ -39,7 +39,7 @@
     conv_gain,
     conv_kernel,
     conv_scale,
-    out,
+    result,
     masked,
     wq,
     wk,
@@ -48,13 +48,13 @@
     normed,
     query,
     window,
+    raw,
     context,
     attended,
     padded,
-    result,
     gains,
+    cells,
     load_sem,
-    out_sem,
     z_send,
     z_recv,
     y_send,
@@ -68,12 +68,19 @@
     wide = width // groups
     me = lax.axis_index("tm")
     odd = lax.rem(me, 2)
-    ahead = lax.rem(me + 2, n)
-    behind = lax.rem(me + n - 2, n)
+    ahead = jnp.minimum(me + 2, n - 1)
+    behind = jnp.maximum(me - 2, 0)
     mate = me + 1 - 2 * odd
-    other = lax.rem(me + n - 1 + 2 * odd, n)
-    after = lax.rem(me + 1, n)
-    before = lax.rem(me + n - 1, n)
+    other = jnp.clip(me - 1 + 2 * odd, 0, n - 1)
+    after = jnp.minimum(me + 1, n - 1)
+    before = jnp.maximum(me - 1, 0)
+    sends_z = me < n - 2
+    gets_z = me >= 2
+    sends_y = me != 1
+    gets_y = me != 0
+    has_before = me > 0
+    has_after = me < n - 1
+    has_other = has_before & has_after
 
     loads = []
     for k, (src, dst) in enumerate(
@@ -84,8 +91,29 @@
         loads.append(copy)
 
     barrier = pltpu.get_barrier_semaphore()
-    for peer in (behind, mate, other):
+
+    def greet(peer):
         pl.semaphore_signal(barrier, inc=1, device_id={"tm": peer}, device_id_type=MESH)
+
+    @pl.when(jnp.logical_not(gets_z))
+    def _():
+        raw[...] = jnp.zeros_like(raw)
+
+        def clear(k, _):
+            window[k, pl.ds(0, 2 * rows)] = jnp.zeros((2 * rows, 2 * GROUP), jnp.bfloat16)
+            return 0
+
+        lax.fori_loop(0, pieces, clear, 0)
+
+    for present, first in ((has_before, 0), (has_after, rows + PAD)):
+
+        @pl.when(jnp.logical_not(present))
+        def _(first=first):
+            padded[:, pl.ds(first, PAD)] = jnp.zeros((recs, PAD, width), jnp.bfloat16)
+
+    greet(mate)
+    pl.when(gets_z)(lambda: greet(behind))
+    pl.when(has_other)(lambda: greet(other))
 
     local = lax.broadcasted_iota(jnp.int32, (rows, 1), 0)
     place = me * rows + local
@@ -99,69 +127,97 @@
             keep = jnp.where(inside, 0.0, keep)
         return keep
 
-    def prepare(r):
-        values = masked[r].astype(jnp.float32)
-        values = values * cut(time_starts, time_widths, r, place)
-        values = values * cut(freq_starts, freq_widths, r, feature)
+    def clean(values, r, places):
+        values = values.astype(jnp.float32)
+        values = values * cut(time_starts, time_widths, r, places)
+        return values * cut(freq_starts, freq_widths, r, feature)
+
+    def prepare(r, _):
+        values = clean(masked[r], r, place)
         masked[r] = values.astype(jnp.bfloat16)
         normed[r] = layer_norm(values, gains[0]).astype(jnp.bfloat16)
+        return 0
 
     for c in range(width // LANES):
         cols = pl.ds(c * LANES, LANES)
         gains[0, :, cols] = attn_gain[pl.ds(c, 1), :]
         gains[1, :, cols] = conv_gain[pl.ds(c, 1), :]
 
-    def z_copy(k):
+    def send(src, dst, sent, got, peer):
         return pltpu.make_async_remote_copy(
-            src_ref=window.at[k, pl.ds(2 * rows, rows)],
-            dst_ref=window.at[k, pl.ds(0, rows)],
-            send_sem=z_send.at[k],
-            recv_sem=z_recv.at[k],
-            device_id={"tm": ahead},
+            src_ref=src,
+            dst_ref=dst,
+            send_sem=sent,
+            recv_sem=got,
+            device_id={"tm": peer},
             device_id_type=MESH,
         )
 
-    def y_copy(k, first):
-        return pltpu.make_async_remote_copy(
-            src_ref=window.at[k, pl.ds(first, rows)],
-            dst_ref=window.at[k, pl.ds(rows, rows)],
-            send_sem=y_send.at[k],
-            recv_sem=y_recv.at[k],
-            device_id={"tm": mate},
-            device_id_type=MESH,
-        )
-
-    def project(r):
-        own = normed[r]
+    def z_copy(k):
+        if isinstance(k, int) and k < groups:
+            src, dst = frames.at[0, :, pl.ds(k * wide, wide)], raw.at[0, k]
+        else:
+            src, dst = window.at[k, pl.ds(2 * rows, rows)], window.at[k, pl.ds(0, rows)]
+        return send(src, dst, z_send.at[k], z_recv.at[k], ahead)
+
+    def y_copy(k, own):
+        if isinstance(k, int) and k < groups:
+            src = frames.at[0, :, pl.ds(k * wide, wide)] if own else raw.at[0, k]
+            dst = raw.at[1, k]
+        else:
+            src = window.at[k, pl.ds(2 * rows if own else 0, rows)]
+            dst = window.at[k, pl.ds(rows, rows)]
+        return send(src, dst, y_send.at[k], y_recv.at[k], mate)
+
+    def relay(k):
+        @pl.when(gets_z)
+        def _():
+            z_copy(k).wait_recv()
+
+        @pl.when((odd == 1) & gets_z)
+        def _():
+            y_copy(k, False).start()
+
+    def launch(k, z_too=True):
+        if z_too:
+
+            @pl.when(sends_z)
+            def _():
+                z_copy(k).start()
+
+        @pl.when(odd == 0)
+        def _():
+            y_copy(k, True).start()
+
+    def project(rows_in, r, first):
         for g in range(groups):
             cols = pl.ds(g * GROUP, GROUP)
             k = r * groups + g
-            window[k, pl.ds(2 * rows, rows), pl.ds(0, GROUP)] = jnp.dot(
-                own, wk[:, cols], preferred_element_type=jnp.float32
+            window[k, pl.ds(first, rows), pl.ds(0, GROUP)] = jnp.dot(
+                rows_in, wk[:, cols], preferred_element_type=jnp.float32
             ).astype(jnp.bfloat16)
-            window[k, pl.ds(2 * rows, rows), pl.ds(GROUP, GROUP)] = jnp.dot(
-                own, wv[:, cols], preferred_element_type=jnp.float32
+            window[k, pl.ds(first, rows), pl.ds(GROUP, GROUP)] = jnp.dot(
+                rows_in, wv[:, cols], preferred_element_type=jnp.float32
             ).astype(jnp.bfloat16)
 
+    def rebuild(side):
+        values = jnp.concatenate([raw[side, j] for j in range(groups)], axis=1)
+        values = clean(values, 0, place - (2 - side) * rows)
+        project(layer_norm(values, gains[0]).astype(jnp.bfloat16), 0, side * rows)
+
+    pl.semaphore_wait(
+        barrier, 1 + sends_z.astype(jnp.int32) + has_other.astype(jnp.int32)
+    )
+    launch(0)
+    launch(1)
     loads[0].wait()
-    prepare(0)
+    lax.fori_loop(0, recs, prepare, 0)
     loads[1].wait()
     loads[2].wait()
-    project(0)
-    pl.semaphore_wait(barrier, 3)
-    for k in range(AHEAD):
-        z_copy(k).start()
-
-    @pl.when(odd == 0)
-    def _():
-        y_copy(0, 2 * rows).start()
-
-    def more(r, _):
-        prepare(r)
-        project(r)
-        return 0
-
-    lax.fori_loop(1, recs, more, 0)
+    for r in range(recs):
+        project(normed[r], r, 2 * rows)
+        relay(r)
+        launch(r + 2)
 
     loads[3].wait()
 
@@ -174,6 +230,16 @@
         return 0
 
     lax.fori_loop(0, recs, ask, 0)
+    rebuild(0)
+    relay(groups)
+    launch(groups + 2)
+
+    @pl.when(gets_y)
+    def _():
+        for j in range(groups):
+            y_copy(j, True).wait_recv()
+
+    rebuild(1)
     loads[4].wait()
 
     heads = GROUP // HSIZE
@@ -227,110 +293,101 @@
         padded[r, pl.ds(PAD, rows)] = layer_norm(
             held.astype(jnp.float32), gains[1]
         ).astype(jnp.bfloat16)
-        halo(r, 0).start()
-        halo(r, 1).start()
-
-    lead = jnp.where(me > 0, 1.0, 0.0)
-    tail = jnp.where(me < n - 1, 1.0, 0.0)
-    strips = rows // 8
-
-    def convolve(r, g):
-        valid = (place < lengths[r]).astype(jnp.float32)
+        pl.when(has_before)(lambda: halo(r, 0).start())
+        pl.when(has_after)(lambda: halo(r, 1).start())
+
+    def convolve(r, g, first, count):
+        valid = (place[first : first + count] < lengths[r]).astype(jnp.float32)
 
         def tile(c, _):
-            cols = pl.ds(pl.multiple_of(g * wide + c * 128, 128), 128)
-            cells = padded[r, :, cols].astype(jnp.float32)
-            cells = jnp.concatenate(
-                [cells[0:PAD] * lead, cells[PAD : PAD + rows], cells[PAD + rows :] * tail], axis=0
+            cols = pl.ds(pl.multiple_of(g * wide + c * LANES, LANES), LANES)
+            cells[c, pl.ds(0, count + 2 * PAD)] = padded[r, pl.ds(first, count + 2 * PAD), cols].astype(jnp.float32)
+            taps = conv_kernel[:, cols]
+            depth = None
+            for k in range(taps.shape[0]):
+                term = taps[k : k + 1] * cells[c, pl.ds(k + 1, count), :]
+                depth = term if depth is None else depth + term
+            held = attended[r, pl.ds(first, count), cols].astype(jnp.float32)
+            gate = depth / (1.0 + jnp.exp(-depth))
+            scale = conv_scale[pl.ds(g * (wide // LANES) + c, 1), :]
+            result[r, pl.ds(first, count), cols] = ((held + scale * gate) * valid).astype(
+                jnp.bfloat16
             )
-            taps = conv_kernel[:, cols]
-            depth = jnp.zeros((rows, 128), jnp.float32)
-            for b in range(8):
-                part = None
-                for a in range(4):
-                    j = 8 * a + b
-                    if j == 0:
-                        continue
-                    term = taps[j - 1 : j] * cells[8 * a : 8 * a + rows + 8]
-                    part = term if part is None else part + term
-                depth = depth + part[b : b + rows]
-            held = attended[r, :, cols].astype(jnp.float32)
-            gate = depth / (1.0 + jnp.exp(-depth))
-            done = (held + conv_scale[pl.ds(g * (wide // LANES) + c, 1), :] * gate) * valid
-            result[r, :, cols] = done.astype(jnp.bfloat16)
             return 0
 
-        lax.fori_loop(0, wide // 128, tile, 0)
-
-    def write(r):
-        return pltpu.make_async_copy(result.at[r], out.at[r], out_sem.at[r])
+        lax.fori_loop(0, wide // LANES, tile, 0)
+
+    def meet(r):
+        pl.when(has_after)(lambda: halo(r, 0).wait_recv())
+        pl.when(has_before)(lambda: halo(r, 1).wait_recv())
 
     def conv_piece(q):
         r = q // groups
         g = lax.rem(q, groups)
-
-        @pl.when(g == 0)
-        def _():
-            halo(r, 0).wait_recv()
-            halo(r, 1).wait_recv()
-
-        convolve(r, g)
-
-        @pl.when(g == groups - 1)
-        def _():
-            write(r).start()
-
-    def step(k, _):
-        @pl.when(k < pieces)
-        def _():
-            z_copy(k).wait_recv()
-
-            @pl.when(k + AHEAD < pieces)
+        pl.when(g == 0)(lambda: meet(r))
+        convolve(r, g, 0, rows)
+
+    def step(p, _):
+        @pl.when((p > 0) & (p + AHEAD < pieces))
+        def _():
+            relay(p + AHEAD)
+
+            @pl.when(p + AHEAD + 2 < pieces)
             def _():
-                z_copy(k + AHEAD).start()
-
-            @pl.when(odd == 1)
-            def _():
-                y_copy(k, 0).start()
-
-            @pl.when((odd == 0) & (k + 1 < pieces))
-            def _():
-                y_copy(k + 1, 2 * rows).start()
-
-        @pl.when(k > 0)
-        def _():
-            p = k - 1
-            y_copy(p, 0).wait_recv()
-            attend(p)
-
-            @pl.when(lax.rem(p, groups) == groups - 1)
-            def _():
-                finish(p // groups)
-
-            @pl.when(p >= LAG)
-            def _():
-                conv_piece(p - LAG)
-
-        return 0
-
-    lax.fori_loop(0, pieces + 1, step, 0)
+                launch(p + AHEAD + 2)
+
+        @pl.when(gets_y & (p >= groups))
+        def _():
+            y_copy(p, True).wait_recv()
+
+        attend(p)
+
+        @pl.when(lax.rem(p, groups) == groups - 1)
+        def _():
+            finish(p // groups)
+
+        @pl.when(p >= LAG)
+        def _():
+            conv_piece(p - LAG)
+
+        return 0
+
+    lax.fori_loop(0, pieces, step, 0)
 
     def rest(q, _):
         conv_piece(q)
         return 0
 
-    lax.fori_loop(pieces - LAG, pieces, rest, 0)
+    lax.fori_loop(pieces - LAG, pieces - groups, rest, 0)
+    last = recs - 1
+
+    def inner(g, _):
+        convolve(last, g, PAD, rows - 2 * PAD)
+        return 0
+
+    lax.fori_loop(0, groups, inner, 0)
+    meet(last)
+
+    def edges(g, _):
+        convolve(last, g, 0, PAD)
+        convolve(last, g, rows - PAD, PAD)
+        return 0
+
+    lax.fori_loop(0, groups, edges, 0)
+
+    for k in range(groups):
+        pl.when(sends_z)(lambda k=k: z_copy(k).wait_send())
+        pl.when(sends_y)(lambda k=k: y_copy(k, True).wait_send())
 
     def settle(k, _):
-        z_copy(k).wait_send()
-        y_copy(k, 0).wait_send()
-        return 0
-
-    lax.fori_loop(0, pieces, settle, 0)
+        pl.when(sends_z)(lambda: z_copy(k).wait_send())
+        pl.when(sends_y)(lambda: y_copy(k, True).wait_send())
+        return 0
+
+    lax.fori_loop(groups, pieces, settle, 0)
     for r in range(recs):
-        halo(r, 0).wait_send()
-        halo(r, 1).wait_send()
-        write(r).wait()
+        pl.when(has_before)(lambda r=r: halo(r, 0).wait_send())
+        pl.when(has_after)(lambda r=r: halo(r, 1).wait_send())
 
 
 def body(
@@ -360,9 +417,9 @@
     dma = pltpu.SemaphoreType.DMA
     return pl.pallas_call(
         functools.partial(kernel, n),
-        out_shape=jax.ShapeDtypeStruct((recs, rows, width), jnp.bfloat16),
+        out_shape=pltpu.VMEM((recs, rows, width), jnp.bfloat16),
         in_specs=[smem] * 5 + [hbm] * 5 + [vmem] * 4,
-        out_specs=hbm,
+        out_specs=vmem,
         scratch_shapes=[
             pltpu.VMEM((recs, rows, width), jnp.bfloat16),
             pltpu.VMEM((width, inner), jnp.bfloat16),
@@ -372,13 +429,13 @@
             pltpu.VMEM((recs, rows, width), jnp.bfloat16),
             pltpu.VMEM((pieces, rows, GROUP), jnp.bfloat16),
             pltpu.VMEM((pieces, 3 * rows, 2 * GROUP), jnp.bfloat16),
+            pltpu.VMEM((2, groups, rows, width // groups), jnp.bfloat16),
             pltpu.VMEM((recs, rows, inner), jnp.bfloat16),
             pltpu.VMEM((recs, rows, width), jnp.bfloat16),
             pltpu.VMEM((recs, rows + 2 * PAD, width), jnp.bfloat16),
-            pltpu.VMEM((recs, rows, width), jnp.bfloat16),
             pltpu.VMEM((2, 1, width), jnp.float32),
+            pltpu.VMEM((width // groups // LANES, rows + 2 * PAD, LANES), jnp.float32),
             dma((5,)),
-            dma((recs,)),
             dma((pieces,)),
             dma((pieces,)),
             dma((pieces,)),

time: 60.6 us -> 53.4 us (0.88)
  the two profiles are of different devices: /device:TPU:16 before, /device:TPU:6 now
where the time goes in v2:
time: 53.4 us; the launch traced here: 53.3 us
  Pallas kernels  52.3 us (98%)
  local copies, waits for them, and re-layouts  1.02 us (2%)
    pallas_call x1, Pallas kernels, body(): pl.pallas_call(functools.partial(kernel, n), out_shape=pltpu.VMEM((recs,...  52.3 us

profile of v2, /device:TPU:6, one launch (start us, length us, event | category | flops | bytes accessed | tf_op | source)
XLA Modules:
  0.0 53.3 jit_solution(14834382121103296720)
XLA Ops:
  0.0 52.3 %layer.1 = bf16[3,128,1536]{2,1,0:T(8,128)(2,1)S(1)} custom-call(s32[2,3]{1,0:T(2,128)} %bitcast.10, s32[2,3]{1,0:T(2,128)} %bitcast.11, s32[2,3]{1,0:T(2,128)} %bitcast.12, s32[2,3]{1,0:T(2,128)} %bitcast.13, s32[3]{0:T(128)} %lengths.1, bf16[3,128,1536]{2,1,0:T(8,128)(2,1)} %frames.1, bf16[1536,768]{1,0:T(8,128)(2,1)} %w_query.1, bf16[1536,768]{1,0:T(8,128)(2,1)} %w_key.1, ...), custom_call_target="tpu_custom_call" | custom-call | tf_op jit(solution)/shard_map/layer/pallas_call | solution.py:418
  52.3 1.0 %copy.16 = bf16[3,128,1536]{2,1,0:T(8,128)(2,1)} copy(bf16[3,128,1536]{2,1,0:T(8,128)(2,1)S(1)} %layer.1) | data formatting | bytes 2359296

commit v3 on v2

v3 whole, which is shorter than its diff:
```python
import functools

import jax
import jax.numpy as jnp
from jax import lax
from jax.experimental import pallas as pl
from jax.experimental.pallas import tpu as pltpu
from jax.sharding import PartitionSpec as P

MESH = pl.DeviceIdType.MESH
HSIZE = 64
GROUP = 256
PAD = 16
LANES = 128


def layer_norm(values, gain):
    center = jnp.mean(values, axis=-1, keepdims=True)
    moved = values - center
    spread = jnp.mean(moved * moved, axis=-1, keepdims=True)
    return moved * lax.rsqrt(spread + 1e-05) * gain


def kernel(
    n,
    time_starts,
    time_widths,
    freq_starts,
    freq_widths,
    lengths,
    frames,
    w_query,
    w_key,
    w_value,
    w_out,
    attn_gain,
    conv_gain,
    conv_kernel,
    conv_scale,
    result,
    masked,
    wq,
    wk,
    wv,
    wo,
    query,
    main,
    side,
    raw,
    context,
    returned,
    attended,
    padded,
    gains,
    cells,
    load_sem,
    z_send,
    z_recv,
    y_send,
    y_recv,
    halo_send,
    halo_recv,
):
    recs, rows, width = masked.shape
    groups = main.shape[0]
    wide = width // groups
    heads = GROUP // HSIZE
    me = lax.axis_index("tm")
    odd = lax.rem(me, 2)
    mine, lent, last = odd, 1 - odd, recs - 1
    ahead = jnp.minimum(me + 2, n - 1)
    behind = jnp.maximum(me - 2, 0)
    mate = me + 1 - 2 * odd
    other = jnp.clip(me - 1 + 2 * odd, 0, n - 1)
    after = jnp.minimum(me + 1, n - 1)
    before = jnp.maximum(me - 1, 0)
    sends_z = me < n - 2
    gets_z = me >= 2
    sends_y = me != 1
    gets_y = me != 0
    has_before = me > 0
    has_after = me < n - 1
    has_other = has_before & has_after

    loads = []
    for k, (src, dst) in enumerate(
        ((frames, masked), (w_key, wk), (w_value, wv), (w_query, wq), (w_out, wo))
    ):
        copy = pltpu.make_async_copy(src, dst, load_sem.at[k])
        copy.start()
        loads.append(copy)

    @pl.when(jnp.logical_not(gets_z))
    def _():
        for g in range(groups):
            main[g, pl.ds(0, 2 * rows)] = jnp.zeros((2 * rows, 2 * GROUP), jnp.bfloat16)
            side[g, pl.ds(0, 2 * rows)] = jnp.zeros((2 * rows, 2 * GROUP), jnp.bfloat16)

    for present, first in ((has_before, 0), (has_after, rows + PAD)):

        @pl.when(jnp.logical_not(present))
        def _(first=first):
            padded[:, pl.ds(first, PAD)] = jnp.zeros((recs, PAD, width), jnp.bfloat16)

    barrier = pltpu.get_barrier_semaphore()

    def greet(peer):
        pl.semaphore_signal(barrier, inc=1, device_id={"tm": peer}, device_id_type=MESH)

    greet(mate)
    pl.when(gets_z)(lambda: greet(behind))
    pl.when(has_other)(lambda: greet(other))

    def send(src, dst, sent, got, peer):
        return pltpu.make_async_remote_copy(
            src_ref=src,
            dst_ref=dst,
            send_sem=sent,
            recv_sem=got,
            device_id={"tm": peer},
            device_id_type=MESH,
        )

    def slot(block):
        return pl.ds(pl.multiple_of(block * rows, rows), rows)

    def z_raw(k):
        src = frames.at[last, :, pl.ds(k * wide, wide)]
        return send(src, raw.at[0, k], z_send.at[k], z_recv.at[k], ahead)

    def z_main(g):
        k = groups + g
        src, dst = main.at[g, slot(3 - odd)], main.at[g, slot(1 - odd)]
        return send(src, dst, z_send.at[k], z_recv.at[k], ahead)

    def z_own(g):
        k = 2 * groups + g
        src, dst = main.at[g, slot(2 + odd)], main.at[g, slot(odd)]
        return send(src, dst, z_send.at[k], z_recv.at[k], ahead)

    def y_raw(k):
        src = frames.at[lent, :, pl.ds(k * wide, wide)]
        return send(src, raw.at[1, k], y_send.at[k], y_recv.at[k], mate)

    def y_back(g):
        k = groups + g
        return send(returned.at[g], context.at[mine, g], y_send.at[k], y_recv.at[k], mate)

    def y_side(g, own):
        k = 2 * groups + g
        src = frames.at[last, :, pl.ds(g * wide, wide)] if own else raw.at[0, g]
        return send(src, raw.at[2, g], y_send.at[k], y_recv.at[k], mate)

    def to_z(copy):
        pl.when(sends_z)(lambda: copy.start())

    def left_z(copy):
        pl.when(sends_z)(lambda: copy.wait_send())

    def from_z(copy):
        pl.when(gets_z)(lambda: copy.wait_recv())

    def relay(g):
        from_z(z_raw(g))
        pl.when((odd == 1) & gets_z)(lambda: y_side(g, False).start())

    pl.semaphore_wait(barrier, 1 + sends_z.astype(jnp.int32) + has_other.astype(jnp.int32))
    for k in range(groups):
        to_z(z_raw(k))
        y_raw(k).start()

    local = lax.broadcasted_iota(jnp.int32, (rows, 1), 0)
    place = me * rows + local
    feature = lax.broadcasted_iota(jnp.int32, (1, width), 1)

    def cut(starts, widths, r, places):
        keep = jnp.ones(places.shape, jnp.float32)
        for m in range(starts.shape[0]):
            first = starts[m, r]
            inside = (places >= first) & (places < first + widths[m, r])
            keep = jnp.where(inside, 0.0, keep)
        return keep

    def clean(values, r, places):
        values = values.astype(jnp.float32)
        values = values * cut(time_starts, time_widths, r, places)
        return values * cut(freq_starts, freq_widths, r, feature)

    for c in range(width // LANES):
        cols = pl.ds(c * LANES, LANES)
        gains[0, :, cols] = attn_gain[pl.ds(c, 1), :]
        gains[1, :, cols] = conv_gain[pl.ds(c, 1), :]

    def project(values, window, block, asks):
        normed = layer_norm(values, gains[0]).astype(jnp.bfloat16)

        def column(g, _):
            cols = pl.ds(pl.multiple_of(g * GROUP, GROUP), GROUP)
            window[g, slot(block), pl.ds(0, GROUP)] = jnp.dot(
                normed, wk[:, cols], preferred_element_type=jnp.float32
            ).astype(jnp.bfloat16)
            window[g, slot(block), pl.ds(GROUP, GROUP)] = jnp.dot(
                normed, wv[:, cols], preferred_element_type=jnp.float32
            ).astype(jnp.bfloat16)
            if asks is not None:
                asked = jnp.dot(normed, wq[:, cols], preferred_element_type=jnp.float32)
                query[asks, g] = asked.astype(jnp.bfloat16) * jnp.bfloat16(HSIZE**-0.5)
            return 0

        for g in range(groups):
            column(g, 0)

    def prepare(r):
        values = clean(masked[r], r, place)
        masked[r] = values.astype(jnp.bfloat16)
        return values

    def rebuild(way, r, shift, window, block, asks):
        values = jnp.concatenate([raw[way, k] for k in range(groups)], axis=1)
        project(clean(values, r, place + shift * rows), window, block, asks)

    loads[0].wait()
    held = prepare(last)
    for k in (1, 2, 3):
        loads[k].wait()
    project(held, side, 2, 2)
    project(prepare(mine), main, 2 + odd, 0)
    prepare(lent)
    for k in range(groups):
        left_z(z_raw(k))
        y_raw(k).wait_send()
    for g in range(groups):
        to_z(z_own(g))
        pl.when(odd == 0)(lambda g=g: y_side(g, True).start())
    for g in range(groups):
        relay(g)
    pl.when(gets_z)(lambda: rebuild(0, last, -2, side, 0, None))
    for k in range(groups):
        y_raw(k).wait_recv()
    rebuild(1, mine, 1 - 2 * odd, main, 3 - odd, 1)
    left_z(z_own(0))
    to_z(z_main(0))
    loads[4].wait()

    head_of = lax.broadcasted_iota(jnp.int32, (1, GROUP), 1) // HSIZE

    def attend(keys, values, asked, length, block):
        stacked = jnp.concatenate(
            [jnp.where(head_of == h, asked, jnp.zeros_like(asked)) for h in range(heads)], axis=0
        )
        score = lax.dot_general(
            stacked, keys, (((1,), (1,)), ((), ())), preferred_element_type=jnp.float32
        )
        key_pos = (block - 2) * rows + lax.broadcasted_iota(jnp.int32, (rows, 3 * rows), 1)
        allowed = (key_pos >= 0) & ((key_pos < length) | (key_pos == block * rows + local))
        allowed = jnp.concatenate([allowed] * heads, axis=0)
        score = jnp.where(allowed, score, -1e30)
        top = jnp.max(score, axis=-1, keepdims=True)
        weights = jnp.exp(score - top)
        total = jnp.sum(weights, axis=-1, keepdims=True)
        mixed = jnp.dot(weights.astype(jnp.bfloat16), values, preferred_element_type=jnp.float32)
        mixed = mixed / total
        own = mixed[0:rows]
        for h in range(1, heads):
            own = jnp.where(head_of == h, mixed[h * rows : (h + 1) * rows], own)
        return own.astype(jnp.bfloat16)

    def attend_main(g, which, asks):
        seen = pl.ds(pl.multiple_of(which * rows, rows), 3 * rows)
        return attend(
            main[g, seen, pl.ds(0, GROUP)],
            main[g, seen, pl.ds(GROUP, GROUP)],
            query[asks, g],
            lengths[mine],
            me - odd + which,
        )

    def attend_side(g):
        context[last, g] = attend(
            side[g, :, pl.ds(0, GROUP)],
            side[g, :, pl.ds(GROUP, GROUP)],
            query[2, g],
            lengths[last],
            me,
        )

    def halo(r, way):
        target = after if way else before
        source = rows if way else PAD
        dest = 0 if way else rows + PAD
        return send(
            padded.at[r, pl.ds(source, PAD)],
            padded.at[r, pl.ds(dest, PAD)],
            halo_send.at[r, way],
            halo_recv.at[r, way],
            target,
        )

    def finish(r):
        mixed = jnp.concatenate([context[r, g] for g in range(groups)], axis=1)
        mixed = jnp.dot(mixed, wo[...], preferred_element_type=jnp.float32)
        valid = (place < lengths[r]).astype(jnp.float32)
        held = ((masked[r].astype(jnp.float32) + mixed) * valid).astype(jnp.bfloat16)
        attended[r] = held
        padded[r, pl.ds(PAD, rows)] = layer_norm(
            held.astype(jnp.float32), gains[1]
        ).astype(jnp.bfloat16)
        pl.when(has_before)(lambda: halo(r, 0).start())
        pl.when(has_after)(lambda: halo(r, 1).start())

    def convolve(spans):
        lives = [
            (place[first : first + count] < lengths[r]).astype(jnp.float32)
            for r, first, count in spans
        ]

        def tile(c, carry):
            cols = pl.ds(pl.multiple_of(c * LANES, LANES), LANES)
            taps = conv_kernel[:, cols]
            scale = conv_scale[pl.ds(c, 1), :]
            for i, (r, first, count) in enumerate(spans):
                cells[c, pl.ds(48 * i, count + 2 * PAD)] = padded[
                    r, pl.ds(first, count + 2 * PAD), cols
                ].astype(jnp.float32)
            depths = [None] * len(spans)
            for k in range(taps.shape[0]):
                tap = taps[k : k + 1]
                for i, (_, _, count) in enumerate(spans):
                    term = tap * cells[c, pl.ds(48 * i + k + 1, count), :]
                    depths[i] = term if k == 0 else depths[i] + term
            for i, (r, first, count) in enumerate(spans):
                depth = depths[i]
                held = attended[r, pl.ds(first, count), cols].astype(jnp.float32)
                gate = depth / (1.0 + jnp.exp(-depth))
                done = (held + scale * gate) * lives[i]
                result[r, pl.ds(first, count), cols] = done.astype(jnp.bfloat16)
            return carry

        lax.fori_loop(0, width // LANES, tile, 0)

    def meet(r):
        pl.when(has_after)(lambda: halo(r, 0).wait_recv())
        pl.when(has_before)(lambda: halo(r, 1).wait_recv())

    def inner(r):
        convolve([(r, PAD, rows - 2 * PAD)])

    def edges(*which):
        convolve([(r, first, PAD) for r in which for first in (0, rows - PAD)])

    def pair(g):
        from_z(z_main(g))
        returned[g] = attend_main(g, 1 - odd, 1)
        y_back(g).start()
        context[mine, g] = attend_main(g, odd, 0)

    left_z(z_own(1))
    to_z(z_main(1))

    @pl.when(gets_y)
    def _():
        for g in range(groups):
            y_side(g, True).wait_recv()
        rebuild(2, last, -1, side, 1, None)

    for g in range(groups):
        attend_side(g)
    finish(last)
    left_z(z_own(2))
    left_z(z_main(0))
    to_z(z_main(2))
    for g in range(groups):
        from_z(z_own(g))
    pair(0)
    inner(last)
    pair(1)
    pair(2)
    finish(mine)
    inner(mine)
    for g in range(groups):
        y_back(g).wait_recv()
    finish(lent)
    inner(lent)
    meet(last)
    meet(mine)
    meet(lent)
    edges(last, mine, lent)

    for g in range(groups):
        if g > 0:
            left_z(z_main(g))
        y_back(g).wait_send()
        pl.when(sends_y)(lambda g=g: y_side(g, True).wait_send())
    for r in range(recs):
        pl.when(has_before)(lambda r=r: halo(r, 0).wait_send())
        pl.when(has_after)(lambda r=r: halo(r, 1).wait_send())


def body(
    frames,
    time_starts,
    time_widths,
    freq_starts,
    freq_widths,
    lengths,
    w_query,
    w_key,
    w_value,
    w_out,
    attn_gain,
    conv_gain,
    conv_kernel,
    conv_scale,
):
    n = lax.axis_size("tm")
    recs, rows, width = frames.shape
    inner = w_query.shape[1]
    groups = inner // GROUP
    smem = pl.BlockSpec(memory_space=pltpu.SMEM)
    vmem = pl.BlockSpec(memory_space=pltpu.VMEM)
    hbm = pl.BlockSpec(memory_space=pl.ANY)
    dma = pltpu.SemaphoreType.DMA
    return pl.pallas_call(
        functools.partial(kernel, n),
        out_shape=pltpu.VMEM((recs, rows, width), jnp.bfloat16),
        in_specs=[smem] * 5 + [hbm] * 5 + [vmem] * 4,
        out_specs=vmem,
        scratch_shapes=[
            pltpu.VMEM((recs, rows, width), jnp.bfloat16),
            pltpu.VMEM((width, inner), jnp.bfloat16),
            pltpu.VMEM((width, inner), jnp.bfloat16),
            pltpu.VMEM((width, inner), jnp.bfloat16),
            pltpu.VMEM((inner, width), jnp.bfloat16),
            pltpu.VMEM((3, groups, rows, GROUP), jnp.bfloat16),
            pltpu.VMEM((groups, 4 * rows, 2 * GROUP), jnp.bfloat16),
            pltpu.VMEM((groups, 3 * rows, 2 * GROUP), jnp.bfloat16),
            pltpu.VMEM((3, groups, rows, width // groups), jnp.bfloat16),
            pltpu.VMEM((recs, groups, rows, GROUP), jnp.bfloat16),
            pltpu.VMEM((groups, rows, GROUP), jnp.bfloat16),
            pltpu.VMEM((recs, rows, width), jnp.bfloat16),
            pltpu.VMEM((recs, rows + 2 * PAD, width), jnp.bfloat16),
            pltpu.VMEM((2, 1, width), jnp.float32),
            pltpu.VMEM((width // LANES, 18 * PAD, LANES), jnp.float32),
            dma((5,)),
            dma((3 * groups,)),
            dma((3 * groups,)),
            dma((3 * groups,)),
            dma((3 * groups,)),
            dma((recs, 2)),
            dma((recs, 2)),
        ],
        compiler_params=pltpu.CompilerParams(
            collective_id=0, has_side_effects=True, vmem_limit_bytes=56 * 1024 * 1024
        ),
        name="layer",
    )(
        time_starts.T,
        time_widths.T,
        freq_starts.T,
        freq_widths.T,
        lengths,
        frames,
        w_query,
        w_key,
        w_value,
        w_out,
        attn_gain.reshape(width // LANES, LANES),
        conv_gain.reshape(width // LANES, LANES),
        conv_kernel,
        conv_scale.reshape(width // LANES, LANES),
    )


def solution(mesh):
    placed = (
        P("rec", "tm", None),
        P("rec", None),
        P("rec", None),
        P("rec", None),
        P("rec", None),
        P("rec"),
        P(),
        P(),
        P(),
        P(),
        P(),
        P(),
        P(),
        P(),
    )
    return jax.shard_map(
        body, mesh=mesh, in_specs=placed, out_specs=P("rec", "tm", None), check_vma=False
    )
```

time: 53.4 us -> 51 us (0.955)
  Pallas kernels: 52.3 us -> 49.8 us
    pallas_call x1, Pallas kernels: 52.3 us -> 49.8 us  [body(): pl.pallas_call(functools.partial(kernel, n), out_shape=pltpu.VMEM((recs,...]
where the time goes in v3:
time: 51 us; the launch traced here: 50.9 us
  Pallas kernels  49.8 us (98%)
  local copies, waits for them, and re-layouts  1.02 us (2%)
    pallas_call x1, Pallas kernels, body(): pl.pallas_call(functools.partial(kernel, n), out_shape=pltpu.VMEM((recs,...  49.8 us

profile of v3, /device:TPU:6, one launch (start us, length us, event | category | flops | bytes accessed | tf_op | source)
XLA Modules:
  0.0 50.9 jit_solution(5329868854834937467)
XLA Ops:
  0.0 49.8 %layer.1 = bf16[3,128,1536]{2,1,0:T(8,128)(2,1)S(1)} custom-call(s32[2,3]{1,0:T(2,128)} %bitcast.10, s32[2,3]{1,0:T(2,128)} %bitcast.11, s32[2,3]{1,0:T(2,128)} %bitcast.12, s32[2,3]{1,0:T(2,128)} %bitcast.13, s32[3]{0:T(128)} %lengths.1, bf16[3,128,1536]{2,1,0:T(8,128)(2,1)} %frames.1, bf16[1536,768]{1,0:T(8,128)(2,1)} %w_query.1, bf16[1536,768]{1,0:T(8,128)(2,1)} %w_key.1, ...), custom_call_target="tpu_custom_call" | custom-call | tf_op jit(solution)/shard_map/layer/pallas_call | solution.py:423
  49.8 1.0 %copy.16 = bf16[3,128,1536]{2,1,0:T(8,128)(2,1)} copy(bf16[3,128,1536]{2,1,0:T(8,128)(2,1)S(1)} %layer.1) | data formatting | bytes 2359296

commit v4 on v3

--- a/solution.py
+++ b/solution.py
@@ -369,10 +369,10 @@
     left_z(z_own(2))
     left_z(z_main(0))
     to_z(z_main(2))
+    inner(last)
     for g in range(groups):
         from_z(z_own(g))
     pair(0)
-    inner(last)
     pair(1)
     pair(2)
     finish(mine)

time: 51 us -> 50.6 us (level)
  no operation moved by 1% of the time
where the time goes in v4:
time: 50.6 us; the launch traced here: 50.5 us
  Pallas kernels  49.5 us (98%)
  local copies, waits for them, and re-layouts  1.02 us (2%)
    pallas_call x1, Pallas kernels, body(): pl.pallas_call(functools.partial(kernel, n), out_shape=pltpu.VMEM((recs,...  49.5 us
    unnamed x1, local copies, waits for them, and re-layouts  1.02 us

profile of v4, /device:TPU:6, one launch (start us, length us, event | category | flops | bytes accessed | tf_op | source)
XLA Modules:
  0.0 50.5 jit_solution(9249052058084757946)
XLA Ops:
  0.0 49.5 %layer.1 = bf16[3,128,1536]{2,1,0:T(8,128)(2,1)S(1)} custom-call(s32[2,3]{1,0:T(2,128)} %bitcast.10, s32[2,3]{1,0:T(2,128)} %bitcast.11, s32[2,3]{1,0:T(2,128)} %bitcast.12, s32[2,3]{1,0:T(2,128)} %bitcast.13, s32[3]{0:T(128)} %lengths.1, bf16[3,128,1536]{2,1,0:T(8,128)(2,1)} %frames.1, bf16[1536,768]{1,0:T(8,128)(2,1)} %w_query.1, bf16[1536,768]{1,0:T(8,128)(2,1)} %w_key.1, ...), custom_call_target="tpu_custom_call" | custom-call | tf_op jit(solution)/shard_map/layer/pallas_call | solution.py:423
  49.5 1.0 %copy.16 = bf16[3,128,1536]{2,1,0:T(8,128)(2,1)} copy(bf16[3,128,1536]{2,1,0:T(8,128)(2,1)S(1)} %layer.1) | data formatting | bytes 2359296

commit v5 on v4

--- a/solution.py
+++ b/solution.py
@@ -352,7 +352,6 @@
         from_z(z_main(g))
         returned[g] = attend_main(g, 1 - odd, 1)
         y_back(g).start()
-        context[mine, g] = attend_main(g, odd, 0)
 
     left_z(z_own(1))
     to_z(z_main(1))
@@ -375,6 +374,8 @@
     pair(0)
     pair(1)
     pair(2)
+    for g in range(groups):
+        context[mine, g] = attend_main(g, odd, 0)
     finish(mine)
     inner(mine)
     for g in range(groups):

time: 50.6 us -> 50.8 us (level)
  no operation moved by 1% of the time
where the time goes in v5:
time: 50.8 us; the launch traced here: 50.7 us
  Pallas kernels  49.7 us (98%)
  local copies, waits for them, and re-layouts  1.02 us (2%)
    pallas_call x1, Pallas kernels, body(): pl.pallas_call(functools.partial(kernel, n), out_shape=pltpu.VMEM((recs,...  49.7 us

profile of v5, /device:TPU:6, one launch (start us, length us, event | category | flops | bytes accessed | tf_op | source)
XLA Modules:
  0.0 50.7 jit_solution(18232783132380710751)
XLA Ops:
  0.0 49.7 %layer.1 = bf16[3,128,1536]{2,1,0:T(8,128)(2,1)S(1)} custom-call(s32[2,3]{1,0:T(2,128)} %bitcast.10, s32[2,3]{1,0:T(2,128)} %bitcast.11, s32[2,3]{1,0:T(2,128)} %bitcast.12, s32[2,3]{1,0:T(2,128)} %bitcast.13, s32[3]{0:T(128)} %lengths.1, bf16[3,128,1536]{2,1,0:T(8,128)(2,1)} %frames.1, bf16[1536,768]{1,0:T(8,128)(2,1)} %w_query.1, bf16[1536,768]{1,0:T(8,128)(2,1)} %w_key.1, ...), custom_call_target="tpu_custom_call" | custom-call | tf_op jit(solution)/shard_map/layer/pallas_call | solution.py:424
  49.7 1.0 %copy.16 = bf16[3,128,1536]{2,1,0:T(8,128)(2,1)} copy(bf16[3,128,1536]{2,1,0:T(8,128)(2,1)S(1)} %layer.1) | data formatting | bytes 2359296
